TPU v7x, 32 devices: a whole 2x2x4 slice. The times are simulated.
32 devices in a mesh: sub: 4 (over y, x), grp: 8 (over z, core).
Axes of the slice: x: 2, y: 2, z: 4, core: 2. Of those that a mesh axis runs over, the one named last changes fastest.
Arguments:
- applied_loads: float32 [4, 8, 64, 1536], P('sub', 'grp')
- flex_matrix: bfloat16 [4, 8, 1536, 1536], P('sub', 'grp'), as said below
- schur_matrix: bfloat16 [4, 8, 1536, 1536], P('sub', 'grp'), as said below
- corner_coupling: float32 [4, 8, 12, 1536], P('sub', 'grp'), may hold values from -0.625 to 0.625
- coarse_inverse: float32 [96, 96], replicated, as said below
- face_match: int32 [4, 8, 4, 384], P('sub', 'grp'), may hold values from 0 to 383, as said below
- corner_map: int32 [4, 8, 12], P('sub', 'grp'), may hold values from 0 to 95, as said below
Outputs:
- multipliers: float32 [4, 8, 64, 4, 384], P('sub', 'grp')
- residual: float32 [4, 8, 64, 4, 384], P('sub', 'grp')
Inputs may be any that keep to these rules, and one draw needn't show every extreme that they name: `flex_matrix`: each subdomain's matrix is symmetric positive definite. `schur_matrix`: each subdomain's matrix is symmetric positive definite. `coarse_inverse`: lower triangular with a positive diagonal. face_match[s, g, 1] is a permutation of the 384 face nodes and face_match[s+1, g, 0] is its inverse; face_match[s, g, 3] and face_match[s, g+1, 2] likewise (indices wrap). `corner_map`: the 12 entries of one subdomain are distinct; every corner unknown is named by exactly four subdomains.
All inputs are finite; a program needn't handle non-finite values.
Results may differ from a plain program's by a relative error of at most 0.0088.
Values sent between devices are 32-bit elements; how exact they have to be, the bound alone decides.
No kernel may reach another device: no remote copies, remote signals or barrier semaphores. Data moves between devices by JAX's collectives and lax.ppermute only.
A program may use at most 64 MiB of HBM per device.

v0:
```python
import jax
import jax.numpy as jnp
from jax import lax
from jax.sharding import PartitionSpec as P

ITERS = 2


def extended(x, sides, width):
    for axis, dim in sides:
        peers, length = (lax.axis_size(axis), x.shape[dim])
        up = [(i, (i + 1) % peers) for i in range(peers)]
        down = [(j, i) for i, j in up]
        last = lax.slice_in_dim(x, length - width, length, axis=dim)
        first = lax.slice_in_dim(x, 0, width, axis=dim)
        before = lax.ppermute(last, axis, up)
        after = lax.ppermute(first, axis, down)
        x = jnp.concatenate([before, x, after], axis=dim)
    return x


def shards(
    applied_loads,
    flex_matrix,
    schur_matrix,
    corner_coupling,
    coarse_inverse,
    face_match,
    corner_map,
):
    highest = lax.Precision.HIGHEST
    load_cases = applied_loads.shape[2]
    interface = applied_loads.shape[3]
    face_size = interface // 4
    flex_local = flex_matrix[0, 0]
    schur_local = schur_matrix[0, 0]
    coupling_local = corner_coupling[0, 0]
    matching = face_match[0, 0]
    corners = corner_map[0, 0]
    coarse_size = coarse_inverse.shape[0]
    selector = (corners[:, None] == jnp.arange(coarse_size, dtype=jnp.int32)[None, :]).astype(
        jnp.float32
    )
    face_signs = jnp.array([-1.0, 1.0, -1.0, 1.0], jnp.float32)[:, None]
    contract_last = (((1,), (1,)), ((), ()))

    def neighbour_jump(displaced):
        around_sub = extended(displaced[:, 0:2], (("sub", 1),), 1)
        around_grp = extended(displaced[:, 2:4], (("grp", 1),), 1)
        from_left_sub = jnp.take(around_sub[:, 0], matching[0], axis=1)
        from_right_sub = jnp.take(around_sub[:, 3], matching[1], axis=1)
        from_left_grp = jnp.take(around_grp[:, 0], matching[2], axis=1)
        from_right_grp = jnp.take(around_grp[:, 3], matching[3], axis=1)
        return jnp.stack(
            [
                from_left_sub - displaced[:, 0],
                displaced[:, 1] - from_right_sub,
                from_left_grp - displaced[:, 2],
                displaced[:, 3] - from_right_grp,
            ],
            axis=1,
        )

    def apply_precond(current):
        weighted = (0.5 * current * face_signs).reshape(load_cases, interface).astype(jnp.bfloat16)
        response = jnp.dot(weighted, schur_local, preferred_element_type=jnp.float32)
        return 0.5 * neighbour_jump(response.reshape(load_cases, 4, face_size))

    def inner(former, latter):
        return lax.psum(0.5 * jnp.sum(former * latter, axis=(1, 2)), ("sub", "grp"))

    right_side = neighbour_jump(applied_loads[0, 0].reshape(load_cases, 4, face_size))
    multipliers = jnp.zeros(right_side.shape, jnp.float32)
    residual = right_side
    precond = apply_precond(residual)
    precond_dot = inner(residual, precond)
    direction = precond
    for iteration in range(ITERS):
        forces = (direction * face_signs).reshape(load_cases, interface)
        apply_free = jnp.dot(
            forces.astype(jnp.bfloat16), flex_local, preferred_element_type=jnp.float32
        )
        corner = lax.dot_general(forces, coupling_local, contract_last, precision=highest)
        share = jnp.dot(corner, selector, precision=highest)
        apply_coarse_total = lax.psum(share, ("sub", "grp"))
        lowered = lax.dot_general(
            apply_coarse_total, coarse_inverse, contract_last, precision=highest
        )
        picked = lax.dot_general(
            jnp.dot(lowered, coarse_inverse, precision=highest),
            selector,
            contract_last,
            precision=highest,
        )
        apply_displaced = apply_free + jnp.dot(picked, coupling_local, precision=highest)
        curvature = lax.psum(jnp.sum(forces * apply_displaced, axis=1), ("sub", "grp"))
        image, curvature = (
            neighbour_jump(apply_displaced.reshape(load_cases, 4, face_size)),
            curvature,
        )
        step_size = (precond_dot / curvature)[:, None, None]
        multipliers = multipliers + step_size * direction
        residual = residual - step_size * image
        if iteration + 1 < ITERS:
            precond = apply_precond(residual)
            next_dot = inner(residual, precond)
            direction = precond + (next_dot / precond_dot)[:, None, None] * direction
            precond_dot = next_dot
    return (multipliers[None, None], residual[None, None])


def solution(mesh):
    return jax.shard_map(
        shards,
        mesh=mesh,
        in_specs=(
            P("sub", "grp", None, None),
            P("sub", "grp", None, None),
            P("sub", "grp", None, None),
            P("sub", "grp", None, None),
            P(),
            P("sub", "grp", None, None),
            P("sub", "grp", None),
        ),
        out_specs=(P("sub", "grp", None, None, None), P("sub", "grp", None, None, None)),
        check_vma=False,
    )
```

profile of v0, /device:TPU:0, one launch (start us, length us, event | category | flops | bytes accessed | tf_op | source)
XLA Modules:
  0.0 294.5 jit_solution(13223852542059288006)
XLA Ops:
  0.6 1.1 reshape_squeeze.3
  2.1 3.0 %collective-permute-start = (f32[64,1,384]{2,0,1:T(8,128)S(1)}, f32[64,1,384]{2,0,1:T(8,128)S(1)}, u32[]{:S(2)}, u32[]{:S(2)}) collective-permute-start(f32[64,1,384]{2,0,1:T(8,128)S(1)} %copy.120), channel_id=1, source_target_pairs={{0,8},{8,16},{16,24},{24,0},{1,9},{9,17},{17,25},{25,1},{2,10},{10... | collective-permute-start | bytes 294920 | tf_op jit(solution)/shard_map/ppermute | solution.py:16
  6.2 3.6 %collective-permute-start.3 = (f32[64,1,384]{2,0,1:T(8,128)S(1)}, f32[64,1,384]{2,0,1:T(8,128)S(1)}, u32[]{:S(2)}, u32[]{:S(2)}) collective-permute-start(f32[64,1,384]{2,0,1:T(8,128)S(1)} %copy.123), channel_id=1, source_target_pairs={{1,0},{2,1},{3,2},{4,3},{5,4},{6,5},{7,6},{0,7},{9,8},{10,9},{11,1... | collective-permute-start | bytes 294920 | tf_op jit(solution)/shard_map/ppermute | solution.py:17
  10.8 6.6 %copy.118 = bf16[1536,1536]{1,0:T(8,128)(2,1)} copy(bf16[1536,1536]{0,1:T(8,128)(2,1)} %bitcast.379) | data formatting | bytes 9437184 | tf_op jit(solution)/shard_map/dot_general | solution.py:66
  17.6 1.1 gather_fusion
  18.9 1.1 gather_fusion.1
  20.3 1.1 gather_fusion.2
  21.7 1.1 gather_fusion.3
  25.9 3.9 %fusion.81 = f32[64,4,384]{2,0,1:T(8,128)S(1)} fusion(bf16[64,1536,1]{1,0,2:T(8,128)(2,1)S(1)} %reshape.865, bf16[4,384,1536]{2,1,0:T(8,128)(2,1)} %bitcast.377), kind=kOutput, calls=%fused_computation.156 | convolution fusion | flops 301989888 | bytes 5308416 | tf_op jit(solution)/shard_map/dot_general | solution.py:66
  29.8 2.1 collective-permute-start.5
  31.9 3.5 %collective-permute-start.7 = (f32[64,1,384]{2,0,1:T(8,128)S(1)}, f32[64,1,384]{2,0,1:T(8,128)S(1)}, u32[]{:S(2)}, u32[]{:S(2)}) collective-permute-start(f32[64,1,384]{2,0,1:T(8,128)S(1)} %get-tuple-element.65), channel_id=1, source_target_pairs={{1,0},{2,1},{3,2},{4,3},{5,4},{6,5},{7,6},{0,7},{9,8},{10,9},{11,1... | collective-permute-start | bytes 294920 | tf_op jit(solution)/shard_map/ppermute | solution.py:17
  35.7 1.1 gather_fusion.5
  36.9 1.6 collective-permute-done.6
  38.6 1.1 gather_fusion.6
  40.0 1.1 gather_fusion.7
  41.4 1.1 gather_fusion.4
  43.7 37.0 %psum.43 = f32[64,96]{1,0:T(8,128)S(1)} all-reduce(f32[64,96]{1,0:T(8,128)S(1)} %fusion.68), channel_id=1, replica_groups=mesh['sub'=4,'grp'=8] {'sub','grp'}, use_global_device_ids=true, to_apply=%region_2.4 | all-reduce | flops 6144 | bytes 49152 | tf_op jit(solution)/shard_map/psum | solution.py:85
  81.9 3.4 %multiply_reduce_fusion.2 = (f32[64]{0:T(128)S(1)}, f32[64,1536]{1,0:T(8,128)S(1)}) fusion(f32[64,1536]{1,0:T(8,128)S(1)} %bitcast.380, f32[1536]{0:T(1024)S(1)} %mul.271, f32[64,1536]{1,0:T(8,128)S(1)} %fusion.20, bf16[64,1536]{1,0:T(8,128)(2,1)S(1)} %bitcast.386, bf16[1,1,1536,1536]{3,2,1,0:T(8,128)(2,1)} %param.11), kind=kOutput, calls=%fused_computation.44 | convolution fusion | flops 302383040 | bytes 6101248 | tf_op jit(solution)/shard_map/dot_general | solution.py:80
  85.7 2.3 collective-permute-start.8
  88.9 3.6 %collective-permute-start.11 = (f32[64,1,384]{2,0,1:T(8,128)S(1)}, f32[64,1,384]{2,0,1:T(8,128)S(1)}, u32[]{:S(2)}, u32[]{:S(2)}) collective-permute-start(f32[64,1,384]{2,0,1:T(8,128)S(1)} %copy.127), channel_id=1, source_target_pairs={{1,0},{2,1},{3,2},{4,3},{5,4},{6,5},{7,6},{0,7},{9,8},{10,9},{11,1... | collective-permute-start | bytes 294920 | tf_op jit(solution)/shard_map/ppermute | solution.py:17
  92.4 39.3 %all-reduce = (f32[64]{0:T(128)S(1)}, f32[64]{0:T(128)S(1)}) all-reduce(f32[64]{0:T(128)S(1)} %broadcast_multiply_fusion.2, f32[64]{0:T(128)S(1)} %get-tuple-element.88), channel_id=1, replica_groups=mesh['sub'=4,'grp'=8] {'sub','grp'}, use_global_device_ids=true, to_apply=%region_1.3 | all-reduce | flops 128 | bytes 1024 | tf_op jit(solution)/shard_map/psum | solution.py:70
  140.3 3.9 %fusion.84 = f32[64,4,384]{2,0,1:T(8,128)S(1)} fusion(bf16[64,1536,1]{1,0,2:T(8,128)(2,1)S(1)} %reshape.866, bf16[4,384,1536]{2,1,0:T(8,128)(2,1)} %bitcast.378), kind=kOutput, calls=%fused_computation.159 | convolution fusion | flops 301989888 | bytes 5308416 | tf_op jit(solution)/shard_map/dot_general | solution.py:66
  144.5 3.5 %collective-permute-start.13 = (f32[64,1,384]{2,0,1:T(8,128)S(1)}, f32[64,1,384]{2,0,1:T(8,128)S(1)}, u32[]{:S(2)}, u32[]{:S(2)}) collective-permute-start(f32[64,1,384]{2,0,1:T(8,128)S(1)} %get-tuple-element.58), channel_id=1, source_target_pairs={{8,0},{16,8},{24,16},{0,24},{9,1},{17,9},{25,17},{1,25},{10,2},{18... | collective-permute-start | bytes 294920 | tf_op jit(solution)/shard_map/ppermute | solution.py:17
  148.4 1.1 gather_fusion.15
  149.6 1.5 collective-permute-done.13
  152.5 1.4 collective-permute-done.14
  156.9 39.2 %psum.45 = f32[64]{0:T(128)S(1)} all-reduce(f32[64]{0:T(128)S(1)} %broadcast_multiply_fusion), channel_id=1, replica_groups=mesh['sub'=4,'grp'=8] {'sub','grp'}, use_global_device_ids=true, to_apply=%region_6.8 | all-reduce | flops 64 | bytes 512 | tf_op jit(solution)/shard_map/psum | solution.py:70
  196.9 39.8 %psum.46 = f32[64,96]{1,0:T(8,128)S(1)} all-reduce(f32[64,96]{1,0:T(8,128)S(1)} %fusion.66), channel_id=1, replica_groups=mesh['sub'=4,'grp'=8] {'sub','grp'}, use_global_device_ids=true, to_apply=%region_7.9 | all-reduce | flops 6144 | bytes 49152 | tf_op jit(solution)/shard_map/psum | solution.py:85
  237.9 3.4 %multiply_reduce_fusion = (f32[64]{0:T(128)S(1)}, f32[64,1536]{1,0:T(8,128)S(1)}) fusion(f32[64,1536]{1,0:T(8,128)S(1)} %bitcast.384, f32[64,1536]{1,0:T(8,128)S(1)} %bitcast.381, f32[1536]{0:T(1024)S(1)} %mul.291, f32[64]{0:T(128)S(1)} %divide_multiply_fusion, f32[64,1536]{1,0:T(8,128)S(1)} %fusion.16, bf16[64,1536]{1,0:T(8,128)(2,1)S(1)} %bitcast.385, ...), kind=kOutput, calls=%fused_computation.40 | convolution fusion | flops 302579648 | bytes 6494720 | tf_op jit(solution)/shard_map/dot_general | solution.py:80
  241.8 2.3 collective-permute-start.16
  245.4 3.6 %collective-permute-start.19 = (f32[64,1,384]{2,0,1:T(8,128)S(1)}, f32[64,1,384]{2,0,1:T(8,128)S(1)}, u32[]{:S(2)}, u32[]{:S(2)}) collective-permute-start(f32[64,1,384]{2,0,1:T(8,128)S(1)} %copy.131), channel_id=1, source_target_pairs={{1,0},{2,1},{3,2},{4,3},{5,4},{6,5},{7,6},{0,7},{9,8},{10,9},{11,1... | collective-permute-start | bytes 294920 | tf_op jit(solution)/shard_map/ppermute | solution.py:17
  248.9 37.6 %psum.47 = f32[64]{0:T(128)S(1)} all-reduce(f32[64]{0:T(128)S(1)} %get-tuple-element.90), channel_id=1, replica_groups=mesh['sub'=4,'grp'=8] {'sub','grp'}, use_global_device_ids=true, to_apply=%region_9.11 | all-reduce | flops 64 | bytes 512 | tf_op jit(solution)/shard_map/psum | solution.py:96
  (190 shorter events, 35.7 us)
Async XLA Ops:
  0.6 80.1 %copy-start = (f32[96,96]{1,0:T(8,128)S(1)}, f32[96,96]{1,0:T(8,128)}, u32[]{:S(2)}) copy-start(f32[96,96]{1,0:T(8,128)} %param.14) | copy-start | bytes 110596
  2.1 15.3 %collective-permute-start = (f32[64,1,384]{2,0,1:T(8,128)S(1)}, f32[64,1,384]{2,0,1:T(8,128)S(1)}, u32[]{:S(2)}, u32[]{:S(2)}) collective-permute-start(f32[64,1,384]{2,0,1:T(8,128)S(1)} %copy.120), channel_id=1, source_target_pairs={{0,8},{8,16},{16,24},{24,0},{1,9},{9,17},{17,25},{25,1},{2,10},{10... | collective-permute-start | bytes 294920 | tf_op jit(solution)/shard_map/ppermute | solution.py:16
  5.1 13.7 %collective-permute-start.1 = (f32[64,1,384]{2,0,1:T(8,128)S(1)}, f32[64,1,384]{2,0,1:T(8,128)S(1)}, u32[]{:S(2)}, u32[]{:S(2)}) collective-permute-start(f32[64,1,384]{2,0,1:T(8,128)S(1)} %copy.121), channel_id=1, source_target_pairs={{8,0},{16,8},{24,16},{0,24},{9,1},{17,9},{25,17},{1,25},{10,2},{18... | collective-permute-start | bytes 294920 | tf_op jit(solution)/shard_map/ppermute | solution.py:17
  6.1 14.1 %collective-permute-start.2 = (f32[64,1,384]{2,0,1:T(8,128)S(1)}, f32[64,1,384]{2,0,1:T(8,128)S(1)}, u32[]{:S(2)}, u32[]{:S(2)}) collective-permute-start(f32[64,1,384]{2,0,1:T(8,128)S(1)} %copy.122), channel_id=1, source_target_pairs={{0,1},{1,2},{2,3},{3,4},{4,5},{5,6},{6,7},{7,0},{8,9},{9,10},{10,1... | collective-permute-start | bytes 294920 | tf_op jit(solution)/shard_map/ppermute | solution.py:16
  6.2 15.4 %collective-permute-start.3 = (f32[64,1,384]{2,0,1:T(8,128)S(1)}, f32[64,1,384]{2,0,1:T(8,128)S(1)}, u32[]{:S(2)}, u32[]{:S(2)}) collective-permute-start(f32[64,1,384]{2,0,1:T(8,128)S(1)} %copy.123), channel_id=1, source_target_pairs={{1,0},{2,1},{3,2},{4,3},{5,4},{6,5},{7,6},{0,7},{9,8},{10,9},{11,1... | collective-permute-start | bytes 294920 | tf_op jit(solution)/shard_map/ppermute | solution.py:17
  17.4 8.2 %copy-start.10 = (f32[4]{0:T(128)S(1)}, f32[4]{0:T(128)}, u32[]{:S(2)}) copy-start(f32[4]{0:T(128)} %constant.24) | copy-start | bytes 52
  29.8 5.7 %collective-permute-start.5 = (f32[64,1,384]{2,0,1:T(8,128)S(1)}, f32[64,1,384]{2,0,1:T(8,128)S(1)}, u32[]{:S(2)}, u32[]{:S(2)}) collective-permute-start(f32[64,1,384]{2,0,1:T(8,128)S(1)} %get-tuple-element.67), channel_id=1, source_target_pairs={{8,0},{16,8},{24,16},{0,24},{9,1},{17,9},{25,17},{1,25},{10,2},{18... | collective-permute-start | bytes 294920 | tf_op jit(solution)/shard_map/ppermute | solution.py:17
  31.9 6.6 %collective-permute-start.6 = (f32[64,1,384]{2,0,1:T(8,128)S(1)}, f32[64,1,384]{2,0,1:T(8,128)S(1)}, u32[]{:S(2)}, u32[]{:S(2)}) collective-permute-start(f32[64,1,384]{2,0,1:T(8,128)S(1)} %get-tuple-element.66), channel_id=1, source_target_pairs={{0,1},{1,2},{2,3},{3,4},{4,5},{5,6},{6,7},{7,0},{8,9},{9,10},{10,1... | collective-permute-start | bytes 294920 | tf_op jit(solution)/shard_map/ppermute | solution.py:16
  31.9 8.0 %collective-permute-start.7 = (f32[64,1,384]{2,0,1:T(8,128)S(1)}, f32[64,1,384]{2,0,1:T(8,128)S(1)}, u32[]{:S(2)}, u32[]{:S(2)}) collective-permute-start(f32[64,1,384]{2,0,1:T(8,128)S(1)} %get-tuple-element.65), channel_id=1, source_target_pairs={{1,0},{2,1},{3,2},{4,3},{5,4},{6,5},{7,6},{0,7},{9,8},{10,9},{11,1... | collective-permute-start | bytes 294920 | tf_op jit(solution)/shard_map/ppermute | solution.py:17
  35.4 5.8 %collective-permute-start.4 = (f32[64,1,384]{2,0,1:T(8,128)S(1)}, f32[64,1,384]{2,0,1:T(8,128)S(1)}, u32[]{:S(2)}, u32[]{:S(2)}) collective-permute-start(f32[64,1,384]{2,0,1:T(8,128)S(1)} %get-tuple-element.64), channel_id=1, source_target_pairs={{0,8},{8,16},{16,24},{24,0},{1,9},{9,17},{17,25},{25,1},{2,10},{10... | collective-permute-start | bytes 294920 | tf_op jit(solution)/shard_map/ppermute | solution.py:16
  36.8 6.2 %copy-start.1 = (f32[1,1,12,1536]{3,1,2,0:T(1,128)S(1)}, f32[1,1,12,1536]{3,1,2,0:T(1,128)}, u32[]{:S(2)}) copy-start(f32[1,1,12,1536]{3,1,2,0:T(1,128)} %param.13) | copy-start | bytes 221188
  85.7 46.0 %collective-permute-start.8 = (f32[64,1,384]{2,0,1:T(8,128)S(1)}, f32[64,1,384]{2,0,1:T(8,128)S(1)}, u32[]{:S(2)}, u32[]{:S(2)}) collective-permute-start(f32[64,1,384]{2,0,1:T(8,128)S(1)} %copy.124), channel_id=1, source_target_pairs={{0,8},{8,16},{16,24},{24,0},{1,9},{9,17},{17,25},{25,1},{2,10},{10... | collective-permute-start | bytes 294920 | tf_op jit(solution)/shard_map/ppermute | solution.py:16
  88.0 45.7 %collective-permute-start.9 = (f32[64,1,384]{2,0,1:T(8,128)S(1)}, f32[64,1,384]{2,0,1:T(8,128)S(1)}, u32[]{:S(2)}, u32[]{:S(2)}) collective-permute-start(f32[64,1,384]{2,0,1:T(8,128)S(1)} %copy.125), channel_id=1, source_target_pairs={{8,0},{16,8},{24,16},{0,24},{9,1},{17,9},{25,17},{1,25},{10,2},{18... | collective-permute-start | bytes 294920 | tf_op jit(solution)/shard_map/ppermute | solution.py:17
  88.8 47.0 %collective-permute-start.10 = (f32[64,1,384]{2,0,1:T(8,128)S(1)}, f32[64,1,384]{2,0,1:T(8,128)S(1)}, u32[]{:S(2)}, u32[]{:S(2)}) collective-permute-start(f32[64,1,384]{2,0,1:T(8,128)S(1)} %copy.126), channel_id=1, source_target_pairs={{0,1},{1,2},{2,3},{3,4},{4,5},{5,6},{6,7},{7,0},{8,9},{9,10},{10,1... | collective-permute-start | bytes 294920 | tf_op jit(solution)/shard_map/ppermute | solution.py:16
  88.9 49.0 %collective-permute-start.11 = (f32[64,1,384]{2,0,1:T(8,128)S(1)}, f32[64,1,384]{2,0,1:T(8,128)S(1)}, u32[]{:S(2)}, u32[]{:S(2)}) collective-permute-start(f32[64,1,384]{2,0,1:T(8,128)S(1)} %copy.127), channel_id=1, source_target_pairs={{1,0},{2,1},{3,2},{4,3},{5,4},{6,5},{7,6},{0,7},{9,8},{10,9},{11,1... | collective-permute-start | bytes 294920 | tf_op jit(solution)/shard_map/ppermute | solution.py:17
  138.0 10.2 %copy-start.12 = (f32[4]{0:T(128)S(1)}, f32[4]{0:T(128)}, u32[]{:S(2)}) copy-start(f32[4]{0:T(128)} %constant.3.clone) | copy-start | bytes 52
  144.2 4.1 %collective-permute-start.15 = (f32[64,1,384]{2,0,1:T(8,128)S(1)}, f32[64,1,384]{2,0,1:T(8,128)S(1)}, u32[]{:S(2)}, u32[]{:S(2)}) collective-permute-start(f32[64,1,384]{2,0,1:T(8,128)S(1)} %get-tuple-element.56), channel_id=1, source_target_pairs={{1,0},{2,1},{3,2},{4,3},{5,4},{6,5},{7,6},{0,7},{9,8},{10,9},{11,1... | collective-permute-start | bytes 294920 | tf_op jit(solution)/shard_map/ppermute | solution.py:17
  144.5 6.6 %collective-permute-start.13 = (f32[64,1,384]{2,0,1:T(8,128)S(1)}, f32[64,1,384]{2,0,1:T(8,128)S(1)}, u32[]{:S(2)}, u32[]{:S(2)}) collective-permute-start(f32[64,1,384]{2,0,1:T(8,128)S(1)} %get-tuple-element.58), channel_id=1, source_target_pairs={{8,0},{16,8},{24,16},{0,24},{9,1},{17,9},{25,17},{1,25},{10,2},{18... | collective-permute-start | bytes 294920 | tf_op jit(solution)/shard_map/ppermute | solution.py:17
  148.0 5.8 %collective-permute-start.14 = (f32[64,1,384]{2,0,1:T(8,128)S(1)}, f32[64,1,384]{2,0,1:T(8,128)S(1)}, u32[]{:S(2)}, u32[]{:S(2)}) collective-permute-start(f32[64,1,384]{2,0,1:T(8,128)S(1)} %get-tuple-element.57), channel_id=1, source_target_pairs={{0,1},{1,2},{2,3},{3,4},{4,5},{5,6},{6,7},{7,0},{8,9},{9,10},{10,1... | collective-permute-start | bytes 294920 | tf_op jit(solution)/shard_map/ppermute | solution.py:16
  148.2 7.0 %collective-permute-start.12 = (f32[64,1,384]{2,0,1:T(8,128)S(1)}, f32[64,1,384]{2,0,1:T(8,128)S(1)}, u32[]{:S(2)}, u32[]{:S(2)}) collective-permute-start(f32[64,1,384]{2,0,1:T(8,128)S(1)} %get-tuple-element.55), channel_id=1, source_target_pairs={{0,8},{8,16},{16,24},{24,0},{1,9},{9,17},{17,25},{25,1},{2,10},{10... | collective-permute-start | bytes 294920 | tf_op jit(solution)/shard_map/ppermute | solution.py:16
  241.8 45.9 %collective-permute-start.16 = (f32[64,1,384]{2,0,1:T(8,128)S(1)}, f32[64,1,384]{2,0,1:T(8,128)S(1)}, u32[]{:S(2)}, u32[]{:S(2)}) collective-permute-start(f32[64,1,384]{2,0,1:T(8,128)S(1)} %copy.128), channel_id=1, source_target_pairs={{0,8},{8,16},{16,24},{24,0},{1,9},{9,17},{17,25},{25,1},{2,10},{10... | collective-permute-start | bytes 294920 | tf_op jit(solution)/shard_map/ppermute | solution.py:16
  244.1 44.9 %collective-permute-start.17 = (f32[64,1,384]{2,0,1:T(8,128)S(1)}, f32[64,1,384]{2,0,1:T(8,128)S(1)}, u32[]{:S(2)}, u32[]{:S(2)}) collective-permute-start(f32[64,1,384]{2,0,1:T(8,128)S(1)} %copy.129), channel_id=1, source_target_pairs={{8,0},{16,8},{24,16},{0,24},{9,1},{17,9},{25,17},{1,25},{10,2},{18... | collective-permute-start | bytes 294920 | tf_op jit(solution)/shard_map/ppermute | solution.py:17
  245.2 48.1 %copy-start.2 = (f32[1,1,64,1,384]{4,2,3,1,0:T(8,128)S(1)}, f32[1,1,64,1,384]{4,2,3,1,0:T(8,128)}, u32[]{:S(2)}) copy-start(f32[1,1,64,1,384]{4,2,3,1,0:T(8,128)} %get-tuple-element.80) | copy-start | bytes 294916
  245.2 48.1 %copy-start.3 = (f32[1,1,64,1,384]{4,2,3,1,0:T(8,128)S(1)}, f32[1,1,64,1,384]{4,2,3,1,0:T(8,128)}, u32[]{:S(2)}) copy-start(f32[1,1,64,1,384]{4,2,3,1,0:T(8,128)} %get-tuple-element.82) | copy-start | bytes 294916
  245.2 48.1 %copy-start.4 = (f32[1,1,64,1,384]{4,2,3,1,0:T(8,128)S(1)}, f32[1,1,64,1,384]{4,2,3,1,0:T(8,128)}, u32[]{:S(2)}) copy-start(f32[1,1,64,1,384]{4,2,3,1,0:T(8,128)} %get-tuple-element.84) | copy-start | bytes 294916
  245.2 48.1 %copy-start.5 = (f32[1,1,64,1,384]{4,2,3,1,0:T(8,128)S(1)}, f32[1,1,64,1,384]{4,2,3,1,0:T(8,128)}, u32[]{:S(2)}) copy-start(f32[1,1,64,1,384]{4,2,3,1,0:T(8,128)} %get-tuple-element.86) | copy-start | bytes 294916
  245.2 48.1 %copy-start.6 = (f32[1,1,64,1,384]{4,2,3,1,0:T(8,128)S(1)}, f32[1,1,64,1,384]{4,2,3,1,0:T(8,128)}, u32[]{:S(2)}) copy-start(f32[1,1,64,1,384]{4,2,3,1,0:T(8,128)} %get-tuple-element.72) | copy-start | bytes 294916
  245.2 48.1 %copy-start.7 = (f32[1,1,64,1,384]{4,2,3,1,0:T(8,128)S(1)}, f32[1,1,64,1,384]{4,2,3,1,0:T(8,128)}, u32[]{:S(2)}) copy-start(f32[1,1,64,1,384]{4,2,3,1,0:T(8,128)} %get-tuple-element.74) | copy-start | bytes 294916
  245.2 48.1 %copy-start.8 = (f32[1,1,64,1,384]{4,2,3,1,0:T(8,128)S(1)}, f32[1,1,64,1,384]{4,2,3,1,0:T(8,128)}, u32[]{:S(2)}) copy-start(f32[1,1,64,1,384]{4,2,3,1,0:T(8,128)} %get-tuple-element.76) | copy-start | bytes 294916
  245.2 48.1 %copy-start.9 = (f32[1,1,64,1,384]{4,2,3,1,0:T(8,128)S(1)}, f32[1,1,64,1,384]{4,2,3,1,0:T(8,128)}, u32[]{:S(2)}) copy-start(f32[1,1,64,1,384]{4,2,3,1,0:T(8,128)} %get-tuple-element.78) | copy-start | bytes 294916
  245.3 45.2 %collective-permute-start.18 = (f32[64,1,384]{2,0,1:T(8,128)S(1)}, f32[64,1,384]{2,0,1:T(8,128)S(1)}, u32[]{:S(2)}, u32[]{:S(2)}) collective-permute-start(f32[64,1,384]{2,0,1:T(8,128)S(1)} %copy.130), channel_id=1, source_target_pairs={{0,1},{1,2},{2,3},{3,4},{4,5},{5,6},{6,7},{7,0},{8,9},{9,10},{10,1... | collective-permute-start | bytes 294920 | tf_op jit(solution)/shard_map/ppermute | solution.py:16
  245.4 46.6 %collective-permute-start.19 = (f32[64,1,384]{2,0,1:T(8,128)S(1)}, f32[64,1,384]{2,0,1:T(8,128)S(1)}, u32[]{:S(2)}, u32[]{:S(2)}) collective-permute-start(f32[64,1,384]{2,0,1:T(8,128)S(1)} %copy.131), channel_id=1, source_target_pairs={{1,0},{2,1},{3,2},{4,3},{5,4},{6,5},{7,6},{0,7},{9,8},{10,9},{11,1... | collective-permute-start | bytes 294920 | tf_op jit(solution)/shard_map/ppermute | solution.py:17
  (1 other events, 5.0 us)
where the time goes:
time: 296 us; the launch traced here: 295 us
  blocking collectives  193 us (65%)
  local copies, waits for them, and re-layouts  39.9 us (13%)
  starting transfers between devices  30.9 us (10%)
  matrix products  17.9 us (6%)
  other arithmetic  6.71 us (2%)
  waiting for transfers between devices  4.44 us (2%)
    psum x2, blocking collectives, inner(): return lax.psum(0.5 * jnp.sum(former * latter, axis=(1, 2)), ('sub', 'grp'))  78.5 us
    psum x2, blocking collectives, shards(): apply_coarse_total = lax.psum(share, ('sub', 'grp'))  76.9 us
    psum x1, blocking collectives, shards(): lax.psum(jnp.sum(forces * apply_displaced, axis=1), ('sub', 'grp'))  37.6 us
    ppermute x10, starting transfers between devices, extended(): after = lax.ppermute(first, axis, down)  23 us
    ppermute x10, starting transfers between devices, extended(): before = lax.ppermute(last, axis, up)  7.96 us
    dot_general x2, matrix products, apply_precond(): jnp.dot(weighted, schur_local, preferred_element_type=jnp.float32)  7.72 us
    dot_general x2, matrix products, shards(): jnp.dot(forces.astype(jnp.bfloat16), flex_local, preferred_element_type=j...  6.8 us
    dot_general x1, local copies, waits for them, and re-layouts, apply_precond(): jnp.dot(weighted, schur_local, preferred_element_type=jnp.float32)  6.62 us
  transfers between devices with their start and end apart: 20, of which 3 were waited for; matrix products, arithmetic and copies ran while one was open for 11% of the time, Pallas kernels for 0%

commit v1 on v0

v1 whole, which is shorter than its diff:
```python
import jax
import jax.numpy as jnp
from jax import lax
from jax.sharding import PartitionSpec as P

HIGHEST = lax.Precision.HIGHEST
LAST = (((1,), (1,)), ((), ()))


def sum_over(values, axis):
    peers = lax.axis_size(axis)
    if peers & (peers - 1):
        return lax.psum(values, axis)
    step = 1
    while step < peers:
        swap = [(i, i ^ step) for i in range(peers)]
        values = values + lax.ppermute(values, axis, swap)
        step *= 2
    return values


def sum_all(values):
    return sum_over(sum_over(values, "grp"), "sub")


def exchange(faces):
    received = []
    for axis, (low, high) in (("sub", faces[0:2]), ("grp", faces[2:4])):
        peers = lax.axis_size(axis)
        up = [(i, (i + 1) % peers) for i in range(peers)]
        down = [(j, i) for i, j in up]
        received.append(lax.ppermute(high, axis, up))
        received.append(lax.ppermute(low, axis, down))
    return received


def split_faces(field):
    size = field.shape[1] // 4
    return [field[:, i * size : (i + 1) * size] for i in range(4)]


def jump(received, own):
    return jnp.concatenate(
        [received[0] - own[0], own[1] - received[1], received[2] - own[2], own[3] - received[3]],
        axis=1,
    )


def two_part_dot(values, matrix):
    high = values.astype(jnp.bfloat16)
    low = (values - high.astype(jnp.float32)).astype(jnp.bfloat16)
    rows = values.shape[0]
    both = jnp.dot(
        jnp.concatenate([high, low], axis=0), matrix, preferred_element_type=jnp.float32
    )
    return both[:rows] + both[rows:]


def shards(
    applied_loads,
    flex_matrix,
    schur_matrix,
    corner_coupling,
    coarse_inverse,
    face_match,
    corner_map,
):
    loads = applied_loads[0, 0]
    flex = flex_matrix[0, 0]
    schur = schur_matrix[0, 0]
    coupling = corner_coupling[0, 0]
    matching = face_match[0, 0]
    corners = corner_map[0, 0]
    cases, interface = loads.shape
    face = interface // 4
    slots = coupling.shape[0]
    coarse_size = coarse_inverse.shape[0]
    signs = jnp.repeat(jnp.array([-1.0, 1.0, -1.0, 1.0], jnp.float32), face)[None, :]

    def matched(received):
        return [jnp.take(received[i], matching[i], axis=1) for i in range(4)]

    def selector(numbers):
        every = jnp.arange(coarse_size, dtype=jnp.int32)
        return (numbers[:, None] == every[None, :]).astype(jnp.float32)

    def spread(numbers, rows):
        return lax.dot_general(
            selector(numbers), rows, (((0,), (0,)), ((), ())), precision=HIGHEST
        )

    numbers = jnp.zeros((1, face), jnp.float32).at[0, :slots].set(corners.astype(jnp.float32))
    own_loads = split_faces(loads)
    own_coupling = split_faces(coupling)
    first = exchange(
        [jnp.concatenate([own_loads[i], own_coupling[i], numbers], axis=0) for i in range(4)]
    )
    first_matched = matched(first)
    residual = jump([x[:cases] for x in first_matched], own_loads)
    own_spread = [spread(corners, x) for x in own_coupling]
    near_spread = [
        spread(
            jnp.round(first[i][cases + slots, :slots]).astype(jnp.int32),
            first_matched[i][cases : cases + slots],
        )
        for i in range(4)
    ]
    coarse_image = jump(near_spread, own_spread)
    own_spread = jnp.concatenate(own_spread, axis=1)

    def precondition(current):
        weighted = (0.5 * current * signs).astype(jnp.bfloat16)
        response = jnp.dot(weighted, schur, preferred_element_type=jnp.float32)
        own = split_faces(response)
        return 0.5 * jump(matched(exchange(own)), own)

    def total(x, y):
        return jnp.sum(x * y, axis=1, keepdims=True)

    def coarse_solve(right):
        lowered = lax.dot_general(right, coarse_inverse, LAST, precision=HIGHEST)
        return jnp.dot(lowered, coarse_inverse, precision=HIGHEST), total(lowered, lowered)

    precond = precondition(residual)
    forces = precond * signs
    free = jnp.dot(forces.astype(jnp.bfloat16), flex, preferred_element_type=jnp.float32)
    sums = sum_all(
        jnp.concatenate(
            [
                lax.dot_general(forces, own_spread, LAST, precision=HIGHEST),
                0.5 * total(residual, precond),
                total(forces, free),
            ],
            axis=1,
        )
    )
    own = split_faces(free)
    free_jump = jump(matched(exchange(own)), own)
    right, rz, local = sums[:, :coarse_size], sums[:, -2:-1], sums[:, -1:]
    coarse, energy = coarse_solve(right)
    curvature = local + energy
    step = rz / curvature
    direction = precond
    multipliers = step * direction
    residual = residual - step * (free_jump + jnp.dot(coarse, coarse_image, precision=HIGHEST))

    precond = precondition(residual)
    forces_next = precond * signs
    free_next = two_part_dot(forces_next, flex)
    sums = sum_all(
        jnp.concatenate(
            [
                lax.dot_general(forces_next, own_spread, LAST, precision=HIGHEST),
                0.5 * total(residual, precond),
                total(forces_next, free_next),
                total(forces_next, free) + total(forces, free_next),
            ],
            axis=1,
        )
    )
    own = split_faces(free_next)
    next_jump = jump(matched(exchange(own)), own)
    beta = sums[:, -3:-2] / rz
    coarse, energy = coarse_solve(sums[:, :coarse_size] + beta * right)
    curvature = sums[:, -2:-1] + beta * sums[:, -1:] + beta * beta * local + energy
    step = sums[:, -3:-2] / curvature
    direction = precond + beta * direction
    image = next_jump + beta * free_jump + jnp.dot(coarse, coarse_image, precision=HIGHEST)
    multipliers = multipliers + step * direction
    residual = residual - step * image
    layout = (1, 1, cases, 4, face)
    return multipliers.reshape(layout), residual.reshape(layout)


def solution(mesh):
    return jax.shard_map(
        shards,
        mesh=mesh,
        in_specs=(
            P("sub", "grp", None, None),
            P("sub", "grp", None, None),
            P("sub", "grp", None, None),
            P("sub", "grp", None, None),
            P(),
            P("sub", "grp", None, None),
            P("sub", "grp", None),
        ),
        out_specs=(P("sub", "grp", None, None, None), P("sub", "grp", None, None, None)),
        check_vma=False,
    )
```

time: 296 us -> 122 us (0.41)
  blocking collectives: 193 us -> 0 us
  waiting for transfers between devices: 4.44 us -> 20 us
  matrix products: 17.9 us -> 21.8 us
    psum x5 -> x0, blocking collectives: 193 us -> none  [the longest x2 78.5 us: inner(): return lax.psum(0.5 * jnp.sum(former * latter, axis=(1, 2)), ('sub', 'grp'))]
    ppermute x20 -> x30, waiting for transfers between devices: 4.44 us -> 20 us  [the longest x10 13.5 us: sum_over(): values = values + lax.ppermute(values, axis, swap)]
    ppermute x0 -> x20, local copies, waits for them, and re-layouts: none -> 7.92 us  [the longest x10 3.97 us: exchange(): received.append(lax.ppermute(low, axis, down))]
    dot_general x1 -> x0, local copies, waits for them, and re-layouts: 6.62 us -> none  [apply_precond(): jnp.dot(weighted, schur_local, preferred_element_type=jnp.float32)]
    dot_general x16 -> x20, matrix products: 17.9 us -> 21.8 us  [the longest x2 6.45 us: precondition(): response = jnp.dot(weighted, schur, preferred_element_type=jnp.float32)]
    another operation x14 -> x2, other arithmetic: 5.51 us -> 1.95 us  [neighbour_jump(): jnp.stack([from_left_sub - displaced[:, 0], displaced[:, 1] - from_right_...]
    ppermute x20 -> x30, starting transfers between devices: 30.9 us -> 32.3 us  [the longest x10 13.2 us: sum_over(): values = values + lax.ppermute(values, axis, swap)]
  transfers between devices with their start and end apart: 20 -> 30, of which waited for: 3 -> 13; matrix products, arithmetic and copies ran while one was open for 11% -> 30% of each run, Pallas kernels for 0% -> 0%
where the time goes in v1:
time: 122 us; the launch traced here: 121 us
  local copies, waits for them, and re-layouts  38.3 us (31%)
  starting transfers between devices  32.3 us (26%)
  matrix products  21.8 us (18%)
  waiting for transfers between devices  20 us (16%)
  other arithmetic  6.99 us (6%)
  between operations  1.71 us (1%)
    gather x40, local copies, waits for them, and re-layouts, matched(): return [jnp.take(received[i], matching[i], axis=1) for i in range(4)]  24.8 us
    ppermute x10, waiting for transfers between devices, sum_over(): values = values + lax.ppermute(values, axis, swap)  13.5 us
    ppermute x10, starting transfers between devices, sum_over(): values = values + lax.ppermute(values, axis, swap)  13.2 us
    ppermute x10, starting transfers between devices, exchange(): received.append(lax.ppermute(low, axis, down))  11.5 us
    ppermute x10, starting transfers between devices, exchange(): received.append(lax.ppermute(high, axis, up))  7.66 us
    dot_general x2, matrix products, precondition(): response = jnp.dot(weighted, schur, preferred_element_type=jnp.float32)  6.45 us
    ppermute x10, waiting for transfers between devices, exchange(): received.append(lax.ppermute(high, axis, up))  5.86 us
    dot_general x8, matrix products, spread(): lax.dot_general(selector(numbers), rows, (((0,), (0,)), ((), ())), precis...  5.28 us
  transfers between devices with their start and end apart: 30, of which 13 were waited for; matrix products, arithmetic and copies ran while one was open for 30% of the time, Pallas kernels for 0%

profile of v1, /device:TPU:0, one launch (start us, length us, event | category | flops | bytes accessed | tf_op | source)
XLA Modules:
  0.0 121.1 jit_solution(466747910016831592)
XLA Ops:
  3.3 1.3 %fusion.52 = f32[1,12]{1,0:T(1,128)S(1)} fusion(pred[]{:T(512)} %compare_reduce_fusion, s32[1,1,12]{2,1,0:T(1,128)} %param.20), kind=kLoop, calls=%fused_computation.159 | loop fusion | flops 24 | bytes 97 | tf_op jit(solution)/shard_map/reshape.186
  4.6 3.0 %collective-permute-start = (f32[77,384]{1,0:T(8,128)S(1)}, f32[77,384]{1,0:T(8,128)S(1)}, u32[]{:S(2)}, u32[]{:S(2)}) collective-permute-start(f32[77,384]{1,0:T(8,128)S(1)} %get-tuple-element.76), channel_id=1, source_target_pairs={{0,8},{8,16},{16,24},{24,0},{1,9},{9,17},{17,25},{25,1},{2,10},{10... | collective-permute-start | bytes 354824 | tf_op jit(solution)/shard_map/ppermute | solution.py:32
  8.6 3.5 %collective-permute-start.3 = (f32[77,384]{1,0:T(8,128)S(1)}, f32[77,384]{1,0:T(8,128)S(1)}, u32[]{:S(2)}, u32[]{:S(2)}) collective-permute-start(f32[77,384]{1,0:T(8,128)S(1)} %get-tuple-element.79), channel_id=1, source_target_pairs={{1,0},{2,1},{3,2},{4,3},{5,4},{6,5},{7,6},{0,7},{9,8},{10,9},{11,1... | collective-permute-start | bytes 354824 | tf_op jit(solution)/shard_map/ppermute | solution.py:33
  18.1 1.1 gather_fusion
  23.7 3.2 %fusion.6 = f32[64,1536]{1,0:T(8,128)S(1)} fusion(bf16[1,1,1536,1536]{3,2,1,0:T(8,128)(2,1)} %param.16, f32[1536]{0:T(1024)S(1)} %mul.200, f32[64,384]{1,0:T(8,128)S(1)} %get-tuple-element.66, f32[64,384]{1,0:T(8,128)S(1)} %get-tuple-element.67, f32[64,384]{1,0:T(8,128)S(1)} %get-tuple-element.65, f32[64,384]{1,0:T(8,128)S(1)} %get-tuple-element.64), kind=kOutput, calls=%fused_computation.26 | convolution fusion | flops 302481408 | bytes 5511168 | tf_op jit(solution)/shard_map/dot_general | solution.py:113
  28.6 1.9 %collective-permute-start.5 = (f32[64,384]{1,0:T(8,128)S(1)}, f32[64,384]{1,0:T(8,128)S(1)}, u32[]{:S(2)}, u32[]{:S(2)}) collective-permute-start(f32[64,384]{1,0:T(8,128)S(1)} %get-tuple-element.63), channel_id=1, source_target_pairs={{8,0},{16,8},{24,16},{0,24},{9,1},{17,9},{25,17},{1,25},{10,2},{18... | collective-permute-start | bytes 294920 | tf_op jit(solution)/shard_map/ppermute | solution.py:33
  31.2 1.9 %collective-permute-done.4 = f32[64,384]{1,0:T(8,128)S(1)} collective-permute-done((f32[64,384]{1,0:T(8,128)S(1)}, f32[64,384]{1,0:T(8,128)S(1)}, u32[]{:S(2)}, u32[]{:S(2)}) %collective-permute-start.4) | collective-permute-done | bytes 98336 | tf_op jit(solution)/shard_map/ppermute | solution.py:32
  34.6 1.1 gather_fusion.7
  36.0 1.1 gather_fusion.6
  38.7 3.4 %multiply_reduce_fusion.5 = (f32[64]{0:T(128)S(1)}, f32[64]{0:T(128)S(1)}, f32[64,1536]{1,0:T(8,128)S(1)}) fusion(f32[64,384]{1,0:T(8,128)S(1)} %get-tuple-element.66, f32[64,384]{1,0:T(8,128)S(1)} %get-tuple-element.67, f32[64,384]{1,0:T(8,128)S(1)} %get-tuple-element.65, f32[64,384]{1,0:T(8,128)S(1)} %get-tuple-element.64, ...), kind=kOutput, calls=%fused_computation.55 | convolution fusion | flops 303660928 | bytes 5904896 | tf_op jit(solution)/shard_map/dot_general | solution.py:126
  44.5 3.9 %collective-permute-done.9 = f32[64,98]{1,0:T(8,128)S(1)} collective-permute-done((f32[64,98]{1,0:T(8,128)S(1)}, f32[64,98]{1,0:T(8,128)S(1)}, u32[]{:S(2)}, u32[]{:S(2)}) %collective-permute-start.9) | collective-permute-done | bytes 25120 | tf_op jit(solution)/shard_map/ppermute | solution.py:17
  50.3 2.3 %collective-permute-start.14 = (f32[64,384]{1,0:T(8,128)S(1)}, f32[64,384]{1,0:T(8,128)S(1)}, u32[]{:S(2)}, u32[]{:S(2)}) collective-permute-start(f32[64,384]{1,0:T(8,128)S(1)} %get-tuple-element.55), channel_id=1, source_target_pairs={{8,0},{16,8},{24,16},{0,24},{9,1},{17,9},{25,17},{1,25},{10,2},{18... | collective-permute-start | bytes 294920 | tf_op jit(solution)/shard_map/ppermute | solution.py:33
  55.0 1.1 gather_fusion.8
  56.3 1.1 gather_fusion.11
  61.1 1.7 %collective-permute-start.12 = (f32[64,98]{1,0:T(8,128)S(1)}, f32[64,98]{1,0:T(8,128)S(1)}, u32[]{:S(2)}, u32[]{:S(2)}) collective-permute-start(f32[64,98]{1,0:T(8,128)S(1)} %add.110), channel_id=1, source_target_pairs={{0,16},{8,24},{16,0},{24,8},{1,17},{9,25},{17,1},{25,9},{2,18},{10... | collective-permute-start | bytes 75272 | tf_op jit(solution)/shard_map/ppermute | solution.py:17
  63.5 1.5 %collective-permute-done.12 = f32[64,98]{1,0:T(8,128)S(1)} collective-permute-done((f32[64,98]{1,0:T(8,128)S(1)}, f32[64,98]{1,0:T(8,128)S(1)}, u32[]{:S(2)}, u32[]{:S(2)}) %collective-permute-start.12) | collective-permute-done | bytes 25120 | tf_op jit(solution)/shard_map/ppermute | solution.py:17
  66.4 3.2 %fusion.4 = f32[64,1536]{1,0:T(8,128)S(1)} fusion(bf16[1,1,1536,1536]{3,2,1,0:T(8,128)(2,1)} %param.16, f32[64,1536]{1,0:T(8,128)S(1)} %multiply_subtract_fusion.1, f32[1536]{0:T(1024)S(1)} %mul.200), kind=kOutput, calls=%fused_computation.24 | convolution fusion | flops 302186496 | bytes 5511168 | tf_op jit(solution)/shard_map/dot_general | solution.py:113
  69.7 1.3 %collective-permute-start.17 = (f32[64,384]{1,0:T(8,128)S(1)}, f32[64,384]{1,0:T(8,128)S(1)}, u32[]{:S(2)}, u32[]{:S(2)}) collective-permute-start(f32[64,384]{1,0:T(8,128)S(1)} %get-tuple-element.44), channel_id=1, source_target_pairs={{0,8},{8,16},{16,24},{24,0},{1,9},{9,17},{17,25},{25,1},{2,10},{10... | collective-permute-start | bytes 294920 | tf_op jit(solution)/shard_map/ppermute | solution.py:32
  71.8 1.8 %collective-permute-start.18 = (f32[64,384]{1,0:T(8,128)S(1)}, f32[64,384]{1,0:T(8,128)}, u32[]{:S(2)}, u32[]{:S(2)}) collective-permute-start(f32[64,384]{1,0:T(8,128)S(1)} %get-tuple-element.47), channel_id=1, source_target_pairs={{8,0},{16,8},{24,16},{0,24},{9,1},{17,9},{25,17},{1,25},{10,2},{18... | collective-permute-start | bytes 294920 | tf_op jit(solution)/shard_map/ppermute | solution.py:33
  73.6 1.7 %collective-permute-done.17 = f32[64,384]{1,0:T(8,128)S(1)} collective-permute-done((f32[64,384]{1,0:T(8,128)S(1)}, f32[64,384]{1,0:T(8,128)S(1)}, u32[]{:S(2)}, u32[]{:S(2)}) %collective-permute-start.17) | collective-permute-done | bytes 98336 | tf_op jit(solution)/shard_map/ppermute | solution.py:32
  75.4 1.1 gather_fusion.12
  80.0 1.1 gather_fusion.14
  85.2 3.1 %fusion = f32[128,1536]{1,0:T(8,128)S(1)} fusion(bf16[1,1,1536,1536]{3,2,1,0:T(8,128)(2,1)} %param.15, bf16[64,1536]{1,0:T(8,128)(2,1)S(1)} %get-tuple-element.37, bf16[64,1536]{1,0:T(8,128)(2,1)S(1)} %get-tuple-element.38), kind=kOutput, calls=%fused_computation.20 | convolution fusion | flops 604766208 | bytes 5898240 | tf_op jit(solution)/shard_map/dot_general | solution.py:53
  89.1 1.2 collective-permute-done.21
  90.3 1.5 %collective-permute-start.22 = (f32[64,99]{1,0:T(8,128)S(1)}, f32[64,99]{1,0:T(8,128)S(1)}, u32[]{:S(2)}, u32[]{:S(2)}) collective-permute-start(f32[64,99]{1,0:T(8,128)S(1)} %fusion.88), channel_id=1, source_target_pairs={{0,2},{1,3},{2,0},{3,1},{4,6},{5,7},{6,4},{7,5},{8,10},{9,11},{10,... | collective-permute-start | bytes 76040 | tf_op jit(solution)/shard_map/ppermute | solution.py:17
  91.9 2.5 %collective-permute-done.22 = f32[64,99]{1,0:T(8,128)S(1)} collective-permute-done((f32[64,99]{1,0:T(8,128)S(1)}, f32[64,99]{1,0:T(8,128)S(1)}, u32[]{:S(2)}, u32[]{:S(2)}) %collective-permute-start.22) | collective-permute-done | bytes 25376 | tf_op jit(solution)/shard_map/ppermute | solution.py:17
  94.3 4.3 %collective-permute-start.23 = (f32[64,99]{1,0:T(8,128)S(1)}, f32[64,99]{1,0:T(8,128)S(1)}, u32[]{:S(2)}, u32[]{:S(2)}) collective-permute-start(f32[64,99]{1,0:T(8,128)S(1)} %add.118), channel_id=1, source_target_pairs={{0,4},{1,5},{2,6},{3,7},{4,0},{5,1},{6,2},{7,3},{8,12},{9,13},{10,... | collective-permute-start | bytes 76040 | tf_op jit(solution)/shard_map/ppermute | solution.py:17
  99.3 1.2 collective-permute-done.23
  100.5 2.3 %collective-permute-start.24 = (f32[64,99]{1,0:T(8,128)S(1)}, f32[64,99]{1,0:T(8,128)S(1)}, u32[]{:S(2)}, u32[]{:S(2)}) collective-permute-start(f32[64,99]{1,0:T(8,128)S(1)} %add.119), channel_id=1, source_target_pairs={{0,8},{8,0},{16,24},{24,16},{1,9},{9,1},{17,25},{25,17},{2,10},{10... | collective-permute-start | bytes 76040 | tf_op jit(solution)/shard_map/ppermute | solution.py:17
  103.2 1.5 %collective-permute-done.26 = f32[64,384]{1,0:T(8,128)} collective-permute-done((f32[64,384]{1,0:T(8,128)S(1)}, f32[64,384]{1,0:T(8,128)}, u32[]{:S(2)}, u32[]{:S(2)}) %collective-permute-start.26) | collective-permute-done | bytes 98336 | tf_op jit(solution)/shard_map/ppermute | solution.py:32
  111.5 2.0 %collective-permute-start.25 = (f32[64,99]{1,0:T(8,128)S(1)}, f32[64,99]{1,0:T(8,128)S(1)}, u32[]{:S(2)}, u32[]{:S(2)}) collective-permute-start(f32[64,99]{1,0:T(8,128)S(1)} %add.120), channel_id=1, source_target_pairs={{0,16},{8,24},{16,0},{24,8},{1,17},{9,25},{17,1},{25,9},{2,18},{10... | collective-permute-start | bytes 76040 | tf_op jit(solution)/shard_map/ppermute | solution.py:17
  113.6 1.9 %collective-permute-done.25 = f32[64,99]{1,0:T(8,128)S(1)} collective-permute-done((f32[64,99]{1,0:T(8,128)S(1)}, f32[64,99]{1,0:T(8,128)S(1)}, u32[]{:S(2)}, u32[]{:S(2)}) %collective-permute-start.25) | collective-permute-done | bytes 25376 | tf_op jit(solution)/shard_map/ppermute | solution.py:17
  (224 shorter events, 54.5 us)
Async XLA Ops:
  0.6 64.4 %copy-start = (f32[96,96]{1,0:T(8,128)S(1)}, f32[96,96]{1,0:T(8,128)}, u32[]{:S(2)}) copy-start(f32[96,96]{1,0:T(8,128)} %param.18) | copy-start | bytes 110596
  4.6 13.3 %collective-permute-start = (f32[77,384]{1,0:T(8,128)S(1)}, f32[77,384]{1,0:T(8,128)S(1)}, u32[]{:S(2)}, u32[]{:S(2)}) collective-permute-start(f32[77,384]{1,0:T(8,128)S(1)} %get-tuple-element.76), channel_id=1, source_target_pairs={{0,8},{8,16},{16,24},{24,0},{1,9},{9,17},{17,25},{25,1},{2,10},{10... | collective-permute-start | bytes 354824 | tf_op jit(solution)/shard_map/ppermute | solution.py:32
  7.6 11.7 %collective-permute-start.1 = (f32[77,384]{1,0:T(8,128)S(1)}, f32[77,384]{1,0:T(8,128)S(1)}, u32[]{:S(2)}, u32[]{:S(2)}) collective-permute-start(f32[77,384]{1,0:T(8,128)S(1)} %get-tuple-element.77), channel_id=1, source_target_pairs={{8,0},{16,8},{24,16},{0,24},{9,1},{17,9},{25,17},{1,25},{10,2},{18... | collective-permute-start | bytes 354824 | tf_op jit(solution)/shard_map/ppermute | solution.py:33
  8.6 12.1 %collective-permute-start.2 = (f32[77,384]{1,0:T(8,128)S(1)}, f32[77,384]{1,0:T(8,128)S(1)}, u32[]{:S(2)}, u32[]{:S(2)}) collective-permute-start(f32[77,384]{1,0:T(8,128)S(1)} %get-tuple-element.78), channel_id=1, source_target_pairs={{0,1},{1,2},{2,3},{3,4},{4,5},{5,6},{6,7},{7,0},{8,9},{9,10},{10,1... | collective-permute-start | bytes 354824 | tf_op jit(solution)/shard_map/ppermute | solution.py:32
  8.6 13.5 %collective-permute-start.3 = (f32[77,384]{1,0:T(8,128)S(1)}, f32[77,384]{1,0:T(8,128)S(1)}, u32[]{:S(2)}, u32[]{:S(2)}) collective-permute-start(f32[77,384]{1,0:T(8,128)S(1)} %get-tuple-element.79), channel_id=1, source_target_pairs={{1,0},{2,1},{3,2},{4,3},{5,4},{6,5},{7,6},{0,7},{9,8},{10,9},{11,1... | collective-permute-start | bytes 354824 | tf_op jit(solution)/shard_map/ppermute | solution.py:33
  27.0 6.1 %collective-permute-start.4 = (f32[64,384]{1,0:T(8,128)S(1)}, f32[64,384]{1,0:T(8,128)S(1)}, u32[]{:S(2)}, u32[]{:S(2)}) collective-permute-start(f32[64,384]{1,0:T(8,128)S(1)} %get-tuple-element.60), channel_id=1, source_target_pairs={{0,8},{8,16},{16,24},{24,0},{1,9},{9,17},{17,25},{25,1},{2,10},{10... | collective-permute-start | bytes 294920 | tf_op jit(solution)/shard_map/ppermute | solution.py:32
  28.0 6.4 %collective-permute-start.7 = (f32[64,384]{1,0:T(8,128)S(1)}, f32[64,384]{1,0:T(8,128)S(1)}, u32[]{:S(2)}, u32[]{:S(2)}) collective-permute-start(f32[64,384]{1,0:T(8,128)S(1)} %get-tuple-element.61), channel_id=1, source_target_pairs={{1,0},{2,1},{3,2},{4,3},{5,4},{6,5},{7,6},{0,7},{9,8},{10,9},{11,1... | collective-permute-start | bytes 294920 | tf_op jit(solution)/shard_map/ppermute | solution.py:33
  28.0 7.8 %collective-permute-start.6 = (f32[64,384]{1,0:T(8,128)S(1)}, f32[64,384]{1,0:T(8,128)S(1)}, u32[]{:S(2)}, u32[]{:S(2)}) collective-permute-start(f32[64,384]{1,0:T(8,128)S(1)} %get-tuple-element.62), channel_id=1, source_target_pairs={{0,1},{1,2},{2,3},{3,4},{4,5},{5,6},{6,7},{7,0},{8,9},{9,10},{10,1... | collective-permute-start | bytes 294920 | tf_op jit(solution)/shard_map/ppermute | solution.py:32
  28.6 8.7 %collective-permute-start.5 = (f32[64,384]{1,0:T(8,128)S(1)}, f32[64,384]{1,0:T(8,128)S(1)}, u32[]{:S(2)}, u32[]{:S(2)}) collective-permute-start(f32[64,384]{1,0:T(8,128)S(1)} %get-tuple-element.63), channel_id=1, source_target_pairs={{8,0},{16,8},{24,16},{0,24},{9,1},{17,9},{25,17},{1,25},{10,2},{18... | collective-permute-start | bytes 294920 | tf_op jit(solution)/shard_map/ppermute | solution.py:33
  31.2 34.7 %copy-start.2 = (f32[96,384]{1,0:T(8,128)}, f32[96,384]{1,0:T(8,128)S(1)}, u32[]{:S(2)}) copy-start(f32[96,384]{1,0:T(8,128)S(1)} %convolution_subtract_fusion.1) | copy-start | bytes 442372
  43.1 1.3 %collective-permute-start.8 = (f32[64,98]{1,0:T(8,128)S(1)}, f32[64,98]{1,0:T(8,128)S(1)}, u32[]{:S(2)}, u32[]{:S(2)}) collective-permute-start(f32[64,98]{1,0:T(8,128)S(1)} %pad_maximum_fusion.11), channel_id=1, source_target_pairs={{0,1},{1,0},{2,3},{3,2},{4,5},{5,4},{6,7},{7,6},{8,9},{9,8},{10,11... | collective-permute-start | bytes 75272 | tf_op jit(solution)/shard_map/ppermute | solution.py:17
  44.4 4.0 %collective-permute-start.9 = (f32[64,98]{1,0:T(8,128)S(1)}, f32[64,98]{1,0:T(8,128)S(1)}, u32[]{:S(2)}, u32[]{:S(2)}) collective-permute-start(f32[64,98]{1,0:T(8,128)S(1)} %fusion.89), channel_id=1, source_target_pairs={{0,2},{1,3},{2,0},{3,1},{4,6},{5,7},{6,4},{7,5},{8,10},{9,11},{10,... | collective-permute-start | bytes 75272 | tf_op jit(solution)/shard_map/ppermute | solution.py:17
  48.4 4.8 %collective-permute-start.10 = (f32[64,98]{1,0:T(8,128)S(1)}, f32[64,98]{1,0:T(8,128)S(1)}, u32[]{:S(2)}, u32[]{:S(2)}) collective-permute-start(f32[64,98]{1,0:T(8,128)S(1)} %add.108), channel_id=1, source_target_pairs={{0,4},{1,5},{2,6},{3,7},{4,0},{5,1},{6,2},{7,3},{8,12},{9,13},{10,... | collective-permute-start | bytes 75272 | tf_op jit(solution)/shard_map/ppermute | solution.py:17
  49.2 5.7 %collective-permute-start.13 = (f32[64,384]{1,0:T(8,128)S(1)}, f32[64,384]{1,0:T(8,128)S(1)}, u32[]{:S(2)}, u32[]{:S(2)}) collective-permute-start(f32[64,384]{1,0:T(8,128)S(1)} %get-tuple-element.52), channel_id=1, source_target_pairs={{0,8},{8,16},{16,24},{24,0},{1,9},{9,17},{17,25},{25,1},{2,10},{10... | collective-permute-start | bytes 294920 | tf_op jit(solution)/shard_map/ppermute | solution.py:32
  49.8 6.4 %collective-permute-start.16 = (f32[64,384]{1,0:T(8,128)S(1)}, f32[64,384]{1,0:T(8,128)S(1)}, u32[]{:S(2)}, u32[]{:S(2)}) collective-permute-start(f32[64,384]{1,0:T(8,128)S(1)} %get-tuple-element.53), channel_id=1, source_target_pairs={{1,0},{2,1},{3,2},{4,3},{5,4},{6,5},{7,6},{0,7},{9,8},{10,9},{11,1... | collective-permute-start | bytes 294920 | tf_op jit(solution)/shard_map/ppermute | solution.py:33
  49.8 7.8 %collective-permute-start.15 = (f32[64,384]{1,0:T(8,128)S(1)}, f32[64,384]{1,0:T(8,128)S(1)}, u32[]{:S(2)}, u32[]{:S(2)}) collective-permute-start(f32[64,384]{1,0:T(8,128)S(1)} %get-tuple-element.54), channel_id=1, source_target_pairs={{0,1},{1,2},{2,3},{3,4},{4,5},{5,6},{6,7},{7,0},{8,9},{9,10},{10,1... | collective-permute-start | bytes 294920 | tf_op jit(solution)/shard_map/ppermute | solution.py:32
  50.3 8.7 %collective-permute-start.14 = (f32[64,384]{1,0:T(8,128)S(1)}, f32[64,384]{1,0:T(8,128)S(1)}, u32[]{:S(2)}, u32[]{:S(2)}) collective-permute-start(f32[64,384]{1,0:T(8,128)S(1)} %get-tuple-element.55), channel_id=1, source_target_pairs={{8,0},{16,8},{24,16},{0,24},{9,1},{17,9},{25,17},{1,25},{10,2},{18... | collective-permute-start | bytes 294920 | tf_op jit(solution)/shard_map/ppermute | solution.py:33
  53.2 7.1 %collective-permute-start.11 = (f32[64,98]{1,0:T(8,128)S(1)}, f32[64,98]{1,0:T(8,128)}, u32[]{:S(2)}, u32[]{:S(2)}) collective-permute-start(f32[64,98]{1,0:T(8,128)S(1)} %add.109), channel_id=1, source_target_pairs={{0,8},{8,0},{16,24},{24,16},{1,9},{9,1},{17,25},{25,17},{2,10},{10... | collective-permute-start | bytes 75272 | tf_op jit(solution)/shard_map/ppermute | solution.py:17
  61.1 3.9 %collective-permute-start.12 = (f32[64,98]{1,0:T(8,128)S(1)}, f32[64,98]{1,0:T(8,128)S(1)}, u32[]{:S(2)}, u32[]{:S(2)}) collective-permute-start(f32[64,98]{1,0:T(8,128)S(1)} %add.110), channel_id=1, source_target_pairs={{0,16},{8,24},{16,0},{24,8},{1,17},{9,25},{17,1},{25,9},{2,18},{10... | collective-permute-start | bytes 75272 | tf_op jit(solution)/shard_map/ppermute | solution.py:17
  69.7 5.6 %collective-permute-start.17 = (f32[64,384]{1,0:T(8,128)S(1)}, f32[64,384]{1,0:T(8,128)S(1)}, u32[]{:S(2)}, u32[]{:S(2)}) collective-permute-start(f32[64,384]{1,0:T(8,128)S(1)} %get-tuple-element.44), channel_id=1, source_target_pairs={{0,8},{8,16},{16,24},{24,0},{1,9},{9,17},{17,25},{25,1},{2,10},{10... | collective-permute-start | bytes 294920 | tf_op jit(solution)/shard_map/ppermute | solution.py:32
  71.0 5.7 %collective-permute-start.20 = (f32[64,384]{1,0:T(8,128)S(1)}, f32[64,384]{1,0:T(8,128)}, u32[]{:S(2)}, u32[]{:S(2)}) collective-permute-start(f32[64,384]{1,0:T(8,128)S(1)} %get-tuple-element.45), channel_id=1, source_target_pairs={{1,0},{2,1},{3,2},{4,3},{5,4},{6,5},{7,6},{0,7},{9,8},{10,9},{11,1... | collective-permute-start | bytes 294920 | tf_op jit(solution)/shard_map/ppermute | solution.py:33
  71.7 7.2 %collective-permute-start.19 = (f32[64,384]{1,0:T(8,128)S(1)}, f32[64,384]{1,0:T(8,128)}, u32[]{:S(2)}, u32[]{:S(2)}) collective-permute-start(f32[64,384]{1,0:T(8,128)S(1)} %get-tuple-element.46), channel_id=1, source_target_pairs={{0,1},{1,2},{2,3},{3,4},{4,5},{5,6},{6,7},{7,0},{8,9},{9,10},{10,1... | collective-permute-start | bytes 294920 | tf_op jit(solution)/shard_map/ppermute | solution.py:32
  71.8 9.5 %collective-permute-start.18 = (f32[64,384]{1,0:T(8,128)S(1)}, f32[64,384]{1,0:T(8,128)}, u32[]{:S(2)}, u32[]{:S(2)}) collective-permute-start(f32[64,384]{1,0:T(8,128)S(1)} %get-tuple-element.47), channel_id=1, source_target_pairs={{8,0},{16,8},{24,16},{0,24},{9,1},{17,9},{25,17},{1,25},{10,2},{18... | collective-permute-start | bytes 294920 | tf_op jit(solution)/shard_map/ppermute | solution.py:33
  89.0 1.3 %collective-permute-start.21 = (f32[64,99]{1,0:T(8,128)S(1)}, f32[64,99]{1,0:T(8,128)S(1)}, u32[]{:S(2)}, u32[]{:S(2)}) collective-permute-start(f32[64,99]{1,0:T(8,128)S(1)} %pad_maximum_fusion.12), channel_id=1, source_target_pairs={{0,1},{1,0},{2,3},{3,2},{4,5},{5,4},{6,7},{7,6},{8,9},{9,8},{10,11... | collective-permute-start | bytes 76040 | tf_op jit(solution)/shard_map/ppermute | solution.py:17
  90.3 4.0 %collective-permute-start.22 = (f32[64,99]{1,0:T(8,128)S(1)}, f32[64,99]{1,0:T(8,128)S(1)}, u32[]{:S(2)}, u32[]{:S(2)}) collective-permute-start(f32[64,99]{1,0:T(8,128)S(1)} %fusion.88), channel_id=1, source_target_pairs={{0,2},{1,3},{2,0},{3,1},{4,6},{5,7},{6,4},{7,5},{8,10},{9,11},{10,... | collective-permute-start | bytes 76040 | tf_op jit(solution)/shard_map/ppermute | solution.py:17
  94.3 6.2 %collective-permute-start.23 = (f32[64,99]{1,0:T(8,128)S(1)}, f32[64,99]{1,0:T(8,128)S(1)}, u32[]{:S(2)}, u32[]{:S(2)}) collective-permute-start(f32[64,99]{1,0:T(8,128)S(1)} %add.118), channel_id=1, source_target_pairs={{0,4},{1,5},{2,6},{3,7},{4,0},{5,1},{6,2},{7,3},{8,12},{9,13},{10,... | collective-permute-start | bytes 76040 | tf_op jit(solution)/shard_map/ppermute | solution.py:17
  98.7 6.0 %collective-permute-start.26 = (f32[64,384]{1,0:T(8,128)S(1)}, f32[64,384]{1,0:T(8,128)}, u32[]{:S(2)}, u32[]{:S(2)}) collective-permute-start(f32[64,384]{1,0:T(8,128)S(1)} %get-tuple-element.32), channel_id=1, source_target_pairs={{0,8},{8,16},{16,24},{24,0},{1,9},{9,17},{17,25},{25,1},{2,10},{10... | collective-permute-start | bytes 294920 | tf_op jit(solution)/shard_map/ppermute | solution.py:32
  98.8 8.1 %collective-permute-start.29 = (f32[64,384]{1,0:T(8,128)S(1)}, f32[64,384]{1,0:T(8,128)}, u32[]{:S(2)}, u32[]{:S(2)}) collective-permute-start(f32[64,384]{1,0:T(8,128)S(1)} %get-tuple-element.33), channel_id=1, source_target_pairs={{1,0},{2,1},{3,2},{4,3},{5,4},{6,5},{7,6},{0,7},{9,8},{10,9},{11,1... | collective-permute-start | bytes 294920 | tf_op jit(solution)/shard_map/ppermute | solution.py:33
  98.8 10.4 %collective-permute-start.28 = (f32[64,384]{1,0:T(8,128)S(1)}, f32[64,384]{1,0:T(8,128)}, u32[]{:S(2)}, u32[]{:S(2)}) collective-permute-start(f32[64,384]{1,0:T(8,128)S(1)} %get-tuple-element.34), channel_id=1, source_target_pairs={{0,1},{1,2},{2,3},{3,4},{4,5},{5,6},{6,7},{7,0},{8,9},{9,10},{10,1... | collective-permute-start | bytes 294920 | tf_op jit(solution)/shard_map/ppermute | solution.py:32
  100.5 11.0 %collective-permute-start.24 = (f32[64,99]{1,0:T(8,128)S(1)}, f32[64,99]{1,0:T(8,128)S(1)}, u32[]{:S(2)}, u32[]{:S(2)}) collective-permute-start(f32[64,99]{1,0:T(8,128)S(1)} %add.119), channel_id=1, source_target_pairs={{0,8},{8,0},{16,24},{24,16},{1,9},{9,1},{17,25},{25,17},{2,10},{10... | collective-permute-start | bytes 76040 | tf_op jit(solution)/shard_map/ppermute | solution.py:17
  111.5 4.0 %collective-permute-start.25 = (f32[64,99]{1,0:T(8,128)S(1)}, f32[64,99]{1,0:T(8,128)S(1)}, u32[]{:S(2)}, u32[]{:S(2)}) collective-permute-start(f32[64,99]{1,0:T(8,128)S(1)} %add.120), channel_id=1, source_target_pairs={{0,16},{8,24},{16,0},{24,8},{1,17},{9,25},{17,1},{25,9},{2,18},{10... | collective-permute-start | bytes 76040 | tf_op jit(solution)/shard_map/ppermute | solution.py:17
  113.6 4.7 %collective-permute-start.27 = (f32[64,384]{1,0:T(8,128)S(1)}, f32[64,384]{1,0:T(8,128)S(1)}, u32[]{:S(2)}, u32[]{:S(2)}) collective-permute-start(f32[64,384]{1,0:T(8,128)S(1)} %get-tuple-element.31), channel_id=1, source_target_pairs={{8,0},{16,8},{24,16},{0,24},{9,1},{17,9},{25,17},{1,25},{10,2},{18... | collective-permute-start | bytes 294920 | tf_op jit(solution)/shard_map/ppermute | solution.py:33
  (20 other events, 340.6 us)
